TPU v7x, 128 devices: a whole 4x4x4 slice. The times are simulated.
128 devices in a mesh: seq: 32 (over y, x, core), head: 4 (over z).
Axes of the slice: x: 4, y: 4, z: 4, core: 2. Of those that a mesh axis runs over, the one named last changes fastest.
Arguments:
- queries: bfloat16 [32768, 8192], P('seq', 'head'), may hold values from -6 to 6
- key_rows: bfloat16 [32768, 8192], P('seq', 'head'), may hold values from -0.5 to 0.5
- value_rows: bfloat16 [32768, 8192], P('seq', 'head'), may hold values from -6 to 6
- log_decay: float32 [64, 32768], P('head', 'seq'), may hold values from -1 to 0, as said below
- gate_logits: bfloat16 [32768, 8192], P(('seq', 'head')), may hold values from -6 to 6
- norm_gain: float32 [8192], replicated, may hold values from 0.5 to 1.5
Outputs:
- gated_out: bfloat16 [32768, 8192], P(('seq', 'head'))
Inputs may be any that keep to these rules, and one draw needn't show every extreme that they name: `log_decay`: log decays are negative.
All inputs are finite; a program needn't handle non-finite values.
Results may differ from a plain program's by a relative error of at most 0.0059.
Values may be sent and summed in bfloat16 or wider, within the bound.
A program may use at most 192 MiB of HBM per device.

v0:
```python
import jax
import jax.numpy as jnp
from jax import lax
from jax.sharding import PartitionSpec as P

BLOCK = 256


norm_eps = 1e-06


def local_states(key_blocks, value_blocks, cumulative):
    block_end = cumulative[:, :, -1]
    key_scale = jnp.exp(block_end[:, :, None] - cumulative).transpose(0, 2, 1)[:, :, :, None]
    weighted_keys = (key_blocks * key_scale).astype(jnp.bfloat16)
    block_state = jnp.einsum(
        "bthd,bthe->bhde", weighted_keys, value_blocks, preferred_element_type=jnp.float32
    )

    def advance(running, inputs):
        decay_end, state_piece = inputs
        return (jnp.exp(decay_end)[:, None, None] * running + state_piece, running)

    empty_state = jnp.zeros(block_state.shape[1:], jnp.float32)
    local_total, local_starts = lax.scan(advance, empty_state, (block_end, block_state))
    return (block_end, local_total, local_starts)


def within_blocks(query_blocks, key_blocks, value_blocks, cumulative):
    scores = jnp.einsum(
        "bthd,bshd->bhts", query_blocks, key_blocks, preferred_element_type=jnp.float32
    )
    length = cumulative.shape[2]
    lower_mask = jnp.tril(jnp.ones((length, length), dtype=bool))[None, None]
    spread = cumulative[:, :, :, None] - cumulative[:, :, None, :]
    weights = jnp.where(
        lower_mask, scores * jnp.exp(jnp.where(lower_mask, spread, 0.0)), 0.0
    ).astype(jnp.bfloat16)
    return jnp.einsum("bhts,bshe->bthe", weights, value_blocks, preferred_element_type=jnp.float32)


def earlier_states(device_decay, local_total):
    totals = lax.all_gather(device_decay[None, :], "seq", axis=0, tiled=True)
    my_index = lax.axis_index("seq")
    inclusive = jnp.cumsum(totals, axis=0)
    shard_ids = jnp.arange(totals.shape[0], dtype=jnp.int32)
    before_here = jnp.sum(
        jnp.where((shard_ids == my_index)[:, None], inclusive - totals, 0.0), axis=0
    )
    shard_piece = lax.all_gather(local_total[None], "seq", axis=0, tiled=True)
    piece_rows = shard_piece.shape[0]
    sources = jnp.arange(piece_rows, dtype=jnp.int32)
    earlier_mask = (sources < my_index)[:, None]
    exponent = jnp.where(earlier_mask, before_here[None, :] - inclusive, 0.0)
    factor = jnp.where(earlier_mask, jnp.exp(exponent), 0.0)
    return jnp.einsum("ph,phde->hde", factor, shard_piece, precision=lax.Precision.HIGHEST)


def on_device(queries, key_rows, value_rows, log_decay, gate_logits, norm_gain):
    local_rows, feature_count = queries.shape
    head_count = log_decay.shape[0]
    head_width = feature_count // head_count
    block_count = local_rows // BLOCK
    query_blocks = queries.reshape(block_count, BLOCK, head_count, head_width)
    key_blocks = key_rows.reshape(block_count, BLOCK, head_count, head_width)
    value_blocks = value_rows.reshape(block_count, BLOCK, head_count, head_width)
    cumulative = jnp.cumsum(log_decay.reshape(head_count, block_count, BLOCK), axis=2).transpose(
        1, 0, 2
    )
    block_end, local_total, local_starts = local_states(key_blocks, value_blocks, cumulative)
    device_decay = jnp.sum(block_end, axis=0)
    incoming = earlier_states(device_decay, local_total)
    within = within_blocks(query_blocks, key_blocks, value_blocks, cumulative)
    decay_before = jnp.cumsum(block_end, axis=0) - block_end
    starts = (jnp.exp(decay_before)[:, :, None, None] * incoming[None] + local_starts).astype(
        jnp.bfloat16
    )
    carried = jnp.einsum(
        "bthd,bhde->bthe", query_blocks, starts, preferred_element_type=jnp.float32
    )
    carried = carried * jnp.exp(cumulative).transpose(0, 2, 1)[:, :, :, None]
    attended = (within + carried).astype(jnp.bfloat16).reshape(local_rows, feature_count)
    token_major = lax.all_to_all(attended, "head", split_axis=0, concat_axis=1, tiled=True)
    widened = token_major.astype(jnp.float32)
    mean_square = jnp.mean(widened * widened, axis=1, keepdims=True)
    normed = widened * lax.rsqrt(mean_square + norm_eps) * norm_gain[None, :]
    return (normed * jax.nn.sigmoid(gate_logits.astype(jnp.float32))).astype(jnp.bfloat16)


def solution(mesh):
    placed = (
        P("seq", "head"),
        P("seq", "head"),
        P("seq", "head"),
        P("head", "seq"),
        P(("seq", "head"), None),
        P(),
    )
    return jax.shard_map(
        on_device, mesh=mesh, in_specs=placed, out_specs=P(("seq", "head"), None), check_vma=False
    )
```

profile of v0, /device:TPU:1, one launch (start us, length us, event | category | flops | bytes accessed | tf_op | source)
XLA Modules:
  0.0 300.1 jit_solution(12429977876080750489)
XLA Ops:
  6.5 0.0 all-gather.4.cloned.1.call-start
  6.5 0.9 reshape.79
  7.5 2.3 reduce-window.6
  9.8 0.2 slice_reduce_fusion
  10.0 0.1 bitcast_bitcast_fusion.1
  10.0 0.2 slice_reduce_fusion.1
  10.3 0.1 fusion.20
  10.4 5.6 %copy.53 = bf16[128,8,16,128]{3,2,1,0:T(8,128)(2,1)} copy(bf16[128,8,16,128]{3,1,2,0:T(8,128)(2,1)} %bitcast.79) | data formatting | bytes 8388608
  16.0 7.4 %copy.41 = bf16[4,256,16,128]{1,3,2,0:T(8,128)(2,1)} copy(bf16[4,256,16,128]{3,2,1,0:T(8,128)(2,1)} %bitcast.74) | data formatting | bytes 8388608 | tf_op jit(solution)/shard_map/reshape | solution.py:65
  23.4 5.6 %copy.54 = bf16[128,8,16,128]{3,2,1,0:T(8,128)(2,1)} copy(bf16[128,8,16,128]{3,1,2,0:T(8,128)(2,1)} %bitcast.80) | data formatting | bytes 8388608
  29.1 7.0 %fusion.6 = f32[4,16,128,128]{3,2,1,0:T(8,128)} fusion(bf16[4,256,16,128]{1,3,2,0:T(8,128)(2,1)} %copy.41, f32[4,256,16]{1,2,0:T(8,128)S(1)} %get-tuple-element.65, bf16[4,256,16,128]{3,2,1,0:T(8,128)(2,1)} %bitcast.72), kind=kOutput, calls=%fused_computation.14 | convolution fusion | flops 543162368 | bytes 12648448 | tf_op jit(solution)/shard_map/bthd,bthe->bhde/dot_general | solution.py:16
  36.0 0.0 copy-start.5
  36.0 10.1 %while.13 = (s32[]{:T(128)}, f32[16,128,128]{2,1,0:T(8,128)S(1)}, f32[4,16,128,128]{3,2,1,0:T(8,128)}, f32[4,16]{1,0:T(4,128)S(1)}, f32[4,16,128,128]{3,2,1,0:T(8,128)}, /*index=5*/s32[]{:T(128)}, s32[]{:T(128)}) while((s32[]{:T(128)}, f32[16,128,128]{2,1,0:T(8,128)S(1)}, f32[4,16,128,128]{3,2,1,0:T(8,128)}, ...), condition=%wide.region_7.8_spmd.clone, body=%wide.region_6.7_spmd.clone.sunk | while | flops 1048579 | bytes 5243680 | solution.py:25
  36.0 1.1 bitcast_dynamic-update-slice_fusion.2
  37.1 1.4 bitcast_add_fusion.2
  38.5 1.1 bitcast_dynamic-update-slice_fusion.2
  39.7 1.4 bitcast_add_fusion.2
  41.1 1.1 bitcast_dynamic-update-slice_fusion.2
  42.2 1.4 bitcast_add_fusion.2
  43.6 1.1 bitcast_dynamic-update-slice_fusion.2
  44.7 1.4 bitcast_add_fusion.2
  46.1 0.0 copy-start
  46.1 1.0 copy-done
  47.1 0.0 all-gather.4.cloned.1.call-update
  47.2 0.0 copy-done.5
  47.2 0.6 dynamic-slice
  48.4 0.2 dynamic-update-slice
  48.6 64.7 %all-reduce = f32[512]{0:T(512)S(1)} all-reduce(f32[512]{0:T(512)S(1)} %dynamic-update-slice), channel_id=2, replica_groups=mesh['seq'=32,'head'=4] {'seq'}, use_global_device_ids=true, to_apply=%add | all-reduce | flops 512 | bytes 4096
  113.4 0.1 reshape.83
  113.5 0.1 reduce_window_sum.43
  113.5 0.1 select_reduce_fusion
  113.6 0.1 select_bitcast_fusion
  113.7 0.1 copy.46
  113.8 5.7 %copy.52 = bf16[128,8,16,128]{3,2,1,0:T(8,128)(2,1)} copy(bf16[128,8,16,128]{3,1,2,0:T(8,128)(2,1)} %bitcast.81) | data formatting | bytes 8388608
  119.5 12.5 %fusion.8 = f32[4,16,256,128]{2,3,1,0:T(8,128)} fusion(bf16[4,256,16,128]{3,2,1,0:T(8,128)(2,1)} %bitcast.73, bf16[4,256,16,128]{1,3,2,0:T(8,128)(2,1)} %copy.41, f32[4,16,256]{2,1,0:T(8,128)S(1)} %bitcast_bitcast_fusion.1, pred[256,256]{1,0:T(8,128)(4,1)S(1)} %iota_compare_fusion, bf16[4,256,16,128]{3,2,1,0:T(8,128)(2,1)} %bitcast.75), kind=kOutput, calls=%fused_computation.17 | convolution fusion | flops 2168455168 | bytes 21102592 | tf_op jit(solution)/shard_map/bhts,bshe->bthe/dot_general | solution.py:39
  132.0 32.9 %all-gather.4.cloned.1.call-done = f32[512,128,128]{2,1,0:T(8,128)} async-done(((f32[16,128,128]{2,1,0:T(8,128)}), f32[512,128,128]{2,1,0:T(8,128)}) %all-gather.4.cloned.1.call-update) | async-done | bytes 33554448 | tf_op jit(solution)/shard_map/all_gather | solution.py:50
  164.9 0.0 copy-start.2
  164.9 43.1 %fusion.2 = f32[16,1,128,128]{3,1,2,0:T(1,128)S(1)} fusion(f32[32,16,1,1]{0,2,3,1:T(1,128)S(1)} %copy.46, f32[32,16,128,128]{3,2,1,0:T(8,128)} %bitcast.70), kind=kOutput, calls=%fused_computation.5 | convolution fusion | flops 100663296 | bytes 34605056 | tf_op jit(solution)/shard_map/ph,phde->hde/dot_general | solution.py:56
  208.0 0.0 copy-done.2
  208.0 9.7 %fusion.5 = bf16[4,256,16,128]{1,3,2,0:T(8,128)(2,1)} fusion(f32[4,16,256,128]{2,3,1,0:T(8,128)} %fusion.8, f32[4,256,16]{1,2,0:T(8,128)S(1)} %get-tuple-element.66, bf16[4,256,16,128]{3,2,1,0:T(8,128)(2,1)S(1)} %bitcast.76, f32[4,16,128,128]{3,2,1,0:T(8,128)} %get-tuple-element.34, f32[16,128,128]{2,1,0:T(8,128)S(1)} %bitcast.78, ...), kind=kOutput, calls=%fused_computation.10 | convolution fusion | flops 546308096 | bytes 22085888 | tf_op jit(solution)/shard_map/bthd,bhde->bthe/dot_general | solution.py:78
  217.7 52.5 %all_to_all.13 = bf16[4,256,2048]{1,2,0:T(8,128)(2,1)S(1)} all-to-all(bf16[4,256,2048]{1,2,0:T(8,128)(2,1)} %bitcast.77), channel_id=1, replica_groups=mesh['seq'=32,'head'=4] {'head'}, dimensions={0} | all-to-all | bytes 8388608 | tf_op jit(solution)/shard_map/all_to_all | solution.py:83
  270.3 0.0 copy-start.1
  270.3 4.3 %convert_element_type.46 = f32[4,256,2048]{1,2,0:T(8,128)} convert(bf16[4,256,2048]{1,2,0:T(8,128)(2,1)S(1)} %all_to_all.13) | non-fusion elementwise | flops 2097152 | bytes 12582912 | tf_op jit(solution)/shard_map/convert_element_type | solution.py:84
  274.6 0.2 copy-done.1
  274.8 0.0 copy-start.4
  274.8 8.9 %copy.50 = f32[256,8192]{1,0:T(8,128)} copy(f32[256,8192]{0,1:T(8,128)} %bitcast.71) | data formatting | bytes 16777216 | tf_op jit(solution)/shard_map/convert_element_type | solution.py:84
  283.7 0.0 copy-start.3
  283.7 3.5 %multiply_reduce_fusion = f32[256]{0:T(256)S(1)} fusion(bf16[4,256,2048]{1,2,0:T(8,128)(2,1)} %copy-done.1), kind=kLoop, calls=%fused_computation.12 | loop fusion | flops 6291200 | bytes 4195328 | tf_op jit(solution)/shard_map/reduce_sum | solution.py:85
  287.2 0.0 copy-done.4
  287.2 0.0 copy-done.3
  287.2 6.0 %multiply_convert_fusion = bf16[256,8192]{1,0:T(8,128)(2,1)} fusion(bf16[256,8192]{1,0:T(8,128)(2,1)S(1)} %copy-done.3, f32[256,8192]{1,0:T(8,128)} %copy.50, f32[8192]{0:T(1024)S(1)} %copy-done.4, f32[256]{0:T(256)S(1)} %add_rsqrt_fusion), kind=kLoop, calls=%fused_computation.11 | loop fusion | flops 16777216 | bytes 16811008 | tf_op jit(solution)/shard_map/convert_element_type | solution.py:87
  (15 shorter events, 0.1 us)
Async XLA Ops:
  6.5 158.4 %all-gather.4.cloned.1.call-start = ((), (), s32[]{:S(2)}) async-start(), calls=%async_computation.1 | async-start | bytes 34603008 | tf_op jit(solution)/shard_map/all_gather | solution.py:50
  36.0 11.1 %copy-start.5 = (u32[128]{0:T(128)S(1)}, u32[128]{0:T(128)}, u32[]{:S(2)}) copy-start(u32[128]{0:T(128)} %constant.44) | copy-start | bytes 1540
  46.1 1.0 copy-start
  164.9 43.1 %copy-start.2 = (bf16[128,8,16,128]{3,2,1,0:T(8,128)(2,1)S(1)}, bf16[128,8,16,128]{3,2,1,0:T(8,128)(2,1)}, u32[]{:S(2)}) copy-start(bf16[128,8,16,128]{3,2,1,0:T(8,128)(2,1)} %copy.52) | copy-start | bytes 12582916
  270.3 4.5 %copy-start.1 = (bf16[4,256,2048]{1,2,0:T(8,128)(2,1)}, bf16[4,256,2048]{1,2,0:T(8,128)(2,1)S(1)}, u32[]{:S(2)}) copy-start(bf16[4,256,2048]{1,2,0:T(8,128)(2,1)S(1)} %all_to_all.13) | copy-start | bytes 12582916
  274.8 12.4 %copy-start.4 = (f32[8192]{0:T(1024)S(1)}, f32[8192]{0:T(1024)}, u32[]{:S(2)}) copy-start(f32[8192]{0:T(1024)} %param.13) | copy-start | bytes 98308
  283.7 3.5 %copy-start.3 = (bf16[256,8192]{1,0:T(8,128)(2,1)S(1)}, bf16[256,8192]{1,0:T(8,128)(2,1)}, u32[]{:S(2)}) copy-start(bf16[256,8192]{1,0:T(8,128)(2,1)} %param.12) | copy-start | bytes 12582916
Sparse Core Ops, SparseCore 0:
  47.2 117.6 all-gather.3
where the time goes:
time: 301 us; the launch traced here: 300 us
  blocking collectives  117 us (39%)
  matrix products  72.3 us (24%)
  local copies, waits for them, and re-layouts  36.6 us (12%)
  waiting for transfers between devices  32.9 us (11%)
  other arithmetic  26.8 us (9%)
  between operations  14.1 us (5%)
    unnamed x1, blocking collectives  64.7 us
    all_to_all x1, blocking collectives, on_device(): lax.all_to_all(attended, 'head', split_axis=0, concat_axis=1, tiled=True)  52.5 us
    dot_general x1, matrix products, earlier_states(): jnp.einsum('ph,phde->hde', factor, shard_piece, precision=lax.Precision.H...  43.1 us
    all_gather x1, waiting for transfers between devices, earlier_states(): shard_piece = lax.all_gather(local_total[None], 'seq', axis=0, tiled=True)  32.9 us
    unnamed x18, local copies, waits for them, and re-layouts  19 us
    dot_general x1, matrix products, within_blocks(): jnp.einsum('bhts,bshe->bthe', weights, value_blocks, preferred_element_ty...  12.5 us
    dot_general x1, matrix products, on_device(): jnp.einsum('bthd,bhde->bthe', query_blocks, starts, preferred_element_typ...  9.73 us
    convert_element_type x1, local copies, waits for them, and re-layouts, on_device(): widened = token_major.astype(jnp.float32)  8.91 us
  transfers between devices with their start and end apart: 1, of which 1 were waited for; matrix products, arithmetic and copies ran while one was open for 7% of the time, Pallas kernels for 0%

commit v1 on v0

v1 whole, which is shorter than its diff:
```python
import jax
import jax.numpy as jnp
from jax import lax
from jax.experimental import pallas as pl
from jax.experimental.pallas import tpu as pltpu
from jax.sharding import PartitionSpec as P

BLOCK = 256
HALF = 128
WIDTH = 128
norm_eps = 1e-06

MESH = pl.DeviceIdType.MESH
F32 = jnp.float32
BF16 = jnp.bfloat16
EXACT = lax.Precision.HIGHEST

NX = 4
NY = 4
AHEAD = 3
LAG_Y = 4
LAG_RET = 7
LAG_ATT = 8
TAIL_PARTS = ((128, 64), (192, 32), (224, 32))


def make_kernel(heads, blocks, z_count):
    groups = heads // 2
    features = heads * WIDTH

    def kernel(
        q_hbm, k_hbm, v_hbm, ld_ref, gate_hbm, gain_ref, out_ref,
        qv, kv, vv, gv, gs, att, recv, cum_row, cum_col, col, loc, start, tot, pair_in, xb, yb, prow, sret, sin,
        dec, dsib, dx, dy,
        load_sem, gate_sem, out_sem, own_sem,
        pair_s, pair_r, x_s, x_r, y_s, y_r, ret_s, ret_r, z_s, z_r,
        dp_s, dp_r, dx_s, dx_r, dy_s, dy_r,
    ):
        seq = lax.axis_index("seq")
        z = lax.axis_index("head")
        core = lax.rem(seq, 2)
        x = lax.rem(seq // 2, NX)
        y = seq // (2 * NX)
        sibling = seq + 1 - 2 * core

        def x_peer(d):
            return (y * NX + lax.rem(x + d, NX)) * 2 + core

        def y_peer(d):
            return (lax.rem(y + d, NY) * NX + x) * 2 + core

        def z_peer(d):
            return lax.rem(z + d, z_count)

        def send(src, dst, s, r, axis, dev):
            return pltpu.make_async_remote_copy(
                src_ref=src, dst_ref=dst, send_sem=s, recv_sem=r, device_id={axis: dev}, device_id_type=MESH
            )

        def load(i, src, dst, h):
            return pltpu.make_async_copy(src.at[:, pl.ds(pl.multiple_of(h * WIDTH, WIDTH), WIDTH)], dst.at[h], load_sem.at[i, h])

        barrier = pltpu.get_barrier_semaphore()
        pl.semaphore_signal(barrier, inc=1, device_id={"seq": sibling}, device_id_type=MESH)
        for d in range(1, NX):
            pl.semaphore_signal(barrier, inc=1, device_id={"seq": x_peer(d)}, device_id_type=MESH)
        for d in range(1, NY):
            pl.semaphore_signal(barrier, inc=1, device_id={"seq": y_peer(d)}, device_id_type=MESH)
        for d in range(1, z_count):
            pl.semaphore_signal(barrier, inc=1, device_id={"head": z_peer(d)}, device_id_type=MESH)

        @pl.loop(0, heads)
        def _(h):
            load(0, k_hbm, kv, h).start()
            load(1, v_hbm, vv, h).start()

        @pl.loop(0, heads)
        def _(h):
            load(2, q_hbm, qv, h).start()

        gate_copy = pltpu.make_async_copy(gate_hbm, gv, gate_sem)
        gate_copy.start()

        t_at = lax.broadcasted_iota(jnp.int32, (BLOCK, BLOCK), 0)
        s_at = lax.broadcasted_iota(jnp.int32, (BLOCK, BLOCK), 1)
        lower = (s_at <= t_at).astype(F32)
        upper = (t_at <= s_at).astype(F32)
        for b in range(blocks):
            ld = ld_ref[:, b * BLOCK : (b + 1) * BLOCK]
            running = jnp.dot(ld, upper, precision=EXACT, preferred_element_type=F32)
            cum_row[b, 0] = running[:, :HALF]
            cum_row[b, 1] = running[:, HALF:]
            padded = jnp.concatenate([ld, jnp.zeros((WIDTH - heads, BLOCK), F32)], axis=0)
            cum_col[b] = lax.dot_general(
                lower, padded, (((1,), (1,)), ((), ())), precision=EXACT, preferred_element_type=F32
            )
        dec[...] = jnp.dot(
            ld_ref[...], jnp.ones((blocks * BLOCK, WIDTH), F32), precision=EXACT, preferred_element_type=F32
        )

        def states(g):
            for i in range(2):
                h = 2 * g + i
                load(0, k_hbm, kv, h).wait()
                load(1, v_hbm, vv, h).wait()

                def block(b, run):
                    turned = pltpu.roll(cum_col[b], lax.rem(WIDTH - h, WIDTH), 1)
                    c = jnp.broadcast_to(turned[:, :1], (BLOCK, WIDTH))
                    col[h, b] = c
                    end = c[BLOCK - 1 :, :]
                    rows = pl.ds(pl.multiple_of(b * BLOCK, BLOCK), BLOCK)
                    weighted = (kv[h, rows, :].astype(F32) * jnp.exp(end - c)).astype(BF16)
                    piece = lax.dot_general(
                        weighted, vv[h, rows, :], (((0,), (0,)), ((), ())), preferred_element_type=F32
                    )
                    loc[h, b] = run
                    return jnp.exp(end) * run + piece

                tot[h] = lax.fori_loop(0, blocks, block, jnp.zeros((WIDTH, WIDTH), F32))

        def pair_copy(g):
            return send(tot.at[2 * g + 1 - core], pair_in.at[g], pair_s.at[g], pair_r.at[g], "seq", sibling)

        def x_copy(g, d):
            return send(xb.at[g, x], xb.at[g, x], x_s.at[g, d - 1], x_r.at[g, d - 1], "seq", x_peer(d))

        def x_got(g, d):
            at = lax.rem(x + NX - d, NX)
            return send(xb.at[g, at], xb.at[g, at], x_s.at[g, d - 1], x_r.at[g, d - 1], "seq", x_peer(d))

        def y_copy(g, d):
            return send(yb.at[g, y], yb.at[g, y], y_s.at[g, d - 1], y_r.at[g, d - 1], "seq", y_peer(d))

        def y_got(g, d):
            at = lax.rem(y + NY - d, NY)
            return send(yb.at[g, at], yb.at[g, at], y_s.at[g, d - 1], y_r.at[g, d - 1], "seq", y_peer(d))

        def ret_copy(g):
            return send(sret.at[g], sin.at[2 * g + core], ret_s.at[g], ret_r.at[g], "seq", sibling)

        def ret_got(g):
            return send(sret.at[g], sin.at[2 * g + 1 - core], ret_s.at[g], ret_r.at[g], "seq", sibling)

        dec_pair = send(dec, dsib, dp_s, dp_r, "seq", sibling)

        def dx_copy(d):
            return send(dx.at[x], dx.at[x], dx_s.at[d - 1], dx_r.at[d - 1], "seq", x_peer(d))

        def dx_got(d):
            at = lax.rem(x + NX - d, NX)
            return send(dx.at[at], dx.at[at], dx_s.at[d - 1], dx_r.at[d - 1], "seq", x_peer(d))

        def dy_copy(d):
            return send(dy.at[y], dy.at[y], dy_s.at[d - 1], dy_r.at[d - 1], "seq", y_peer(d))

        def dy_got(d):
            at = lax.rem(y + NY - d, NY)
            return send(dy.at[at], dy.at[at], dy_s.at[d - 1], dy_r.at[d - 1], "seq", y_peer(d))

        def between(rows, lo, hi):
            total = jnp.zeros((1, WIDTH), F32)
            for i in range(lo + 1, len(rows)):
                total = total + jnp.where(i < hi, rows[i], 0.0)
            return total

        def own_core(g):
            h = 2 * g + core
            mine, other = tot[h], pair_in[g]
            here, there = dec[pl.ds(h, 1), :], dsib[pl.ds(h, 1), :]
            first = core == 0
            return (
                h,
                jnp.where(first, mine, other),
                jnp.where(first, other, mine),
                jnp.where(first, here, there),
                jnp.where(first, there, here),
            )

        def pair_step(g):
            pair_copy(g).wait_recv()

            @pl.when(g == 0)
            def _():
                dec_pair.wait_recv()
                dx[x] = dec[...] + dsib[...]
                for d in range(1, NX):
                    dx_copy(d).start()

            h, first, second, _, second_decay = own_core(g)
            xb[g, x] = (jnp.exp(second_decay) * first + second).astype(xb.dtype)
            for d in range(1, NX):
                x_copy(g, d).start()

        def x_rows(h):
            return [dx[i, pl.ds(h, 1), :] for i in range(NX)]

        def row_step(g):
            @pl.when(g == 0)
            def _():
                for d in range(1, NX):
                    dx_got(d).wait_recv()
                dy[y] = dx[0] + dx[1] + dx[2] + dx[3]
                for d in range(1, NY):
                    dy_copy(d).start()

            for d in range(1, NX):
                x_got(g, d).wait_recv()
            h = 2 * g + core
            rows = x_rows(h)
            whole = jnp.zeros((WIDTH, WIDTH), F32)
            before = jnp.zeros((WIDTH, WIDTH), F32)
            for i in range(NX):
                piece = xb[g, i].astype(F32)
                whole = whole + jnp.exp(between(rows, i, NX)) * piece
                before = before + jnp.where(i < x, jnp.exp(between(rows, i, x)), 0.0) * piece
            prow[g] = before
            yb[g, y] = whole.astype(yb.dtype)
            for d in range(1, NY):
                y_copy(g, d).start()

        def return_step(g):
            @pl.when(g == 0)
            def _():
                for d in range(1, NY):
                    dy_got(d).wait_recv()

            for d in range(1, NY):
                y_got(g, d).wait_recv()
            h, first, _, first_decay, _ = own_core(g)
            rows = [dy[i, pl.ds(h, 1), :] for i in range(NY)]
            above = jnp.zeros((WIDTH, WIDTH), F32)
            for i in range(NY):
                above = above + jnp.where(i < y, jnp.exp(between(rows, i, y)), 0.0) * yb[g, i].astype(F32)
            at_first = jnp.exp(between(x_rows(h), -1, x)) * above + prow[g]
            at_second = jnp.exp(first_decay) * at_first + first
            sin[h] = jnp.where(core == 0, at_first, at_second)
            sret[g] = jnp.where(core == 0, at_second, at_first)
            ret_copy(g).start()

        def z_copy(g, part, r0, rows, d):
            p = z_peer(d)
            src = pl.ds(pl.multiple_of(g * 2 * WIDTH, 2 * WIDTH), 2 * WIDTH)
            dst = pl.ds(pl.multiple_of(z * features + g * 2 * WIDTH, 2 * WIDTH), 2 * WIDTH)
            return send(
                att.at[p, pl.ds(r0, rows), src], recv.at[pl.ds(r0, rows), dst],
                z_s.at[part, g, d - 1], z_r.at[part, g, d - 1], "head", p,
            )

        def z_got(g, part, r0, rows, d):
            src = pl.ds(pl.multiple_of(g * 2 * WIDTH, 2 * WIDTH), 2 * WIDTH)
            origin = lax.rem(z + z_count - d, z_count)
            dst = pl.ds(pl.multiple_of(origin * features + g * 2 * WIDTH, 2 * WIDTH), 2 * WIDTH)
            return send(
                att.at[z_peer(d), pl.ds(r0, rows), src], recv.at[pl.ds(r0, rows), dst],
                z_s.at[part, g, d - 1], z_r.at[part, g, d - 1], "head", z_peer(d),
            )

        def own_copy(g, part, r0, rows):
            src = pl.ds(pl.multiple_of(g * 2 * WIDTH, 2 * WIDTH), 2 * WIDTH)
            dst = pl.ds(pl.multiple_of(z * features + g * 2 * WIDTH, 2 * WIDTH), 2 * WIDTH)
            return pltpu.make_async_copy(
                att.at[z, pl.ds(r0, rows), src], recv.at[pl.ds(r0, rows), dst], own_sem.at[part, g]
            )

        def ship(g, part, r0, rows):
            for d in (2, 1, 3):
                z_copy(g, part, r0, rows, d).start()
            own_copy(g, part, r0, rows).start()

        def arrived(part, r0, rows):
            @pl.loop(0, groups)
            def _(g):
                for d in range(1, z_count):
                    z_got(g, part, r0, rows, d).wait_recv()
                own_copy(g, part, r0, rows).wait()

        def attend_first(g):
            ret_got(g).wait_recv()
            for i in range(2):
                h = 2 * g + i
                load(2, q_hbm, qv, h).wait()

                def block(b, gone):
                    c = col[h, b, :HALF, :]
                    begin = (jnp.exp(gone) * sin[h] + loc[h, b]).astype(BF16)
                    start[h, b] = begin
                    rows = pl.ds(pl.multiple_of(b * BLOCK, BLOCK), HALF)
                    q = qv[h, rows, :]
                    scores = lax.dot_general(q, kv[h, rows, :], (((1,), (1,)), ((), ())), preferred_element_type=F32)
                    keep = lax.broadcasted_iota(jnp.int32, (HALF, HALF), 1) <= lax.broadcasted_iota(
                        jnp.int32, (HALF, HALF), 0
                    )
                    spread = jnp.where(keep, c - cum_row[b, 0, pl.ds(h, 1), :], 0.0)
                    weights = jnp.where(keep, scores * jnp.exp(spread), 0.0).astype(BF16)
                    within = jnp.dot(weights, vv[h, rows, :], preferred_element_type=F32)
                    carried = jnp.dot(q, begin, preferred_element_type=F32) * jnp.exp(c)
                    att[b, :HALF, pl.ds(pl.multiple_of(h * WIDTH, WIDTH), WIDTH)] = (within + carried).astype(BF16)
                    return gone + col[h, b, BLOCK - 1 :, :]

                lax.fori_loop(0, blocks, block, jnp.zeros((1, WIDTH), F32))
            ship(g, 0, 0, HALF)

        def attend_second(g):
            for i in range(2):
                h = 2 * g + i

                @pl.loop(0, blocks)
                def _(b):
                    c = col[h, b, HALF:, :]
                    top = pl.multiple_of(b * BLOCK, BLOCK)
                    rows = pl.ds(top, BLOCK)
                    q = qv[h, pl.ds(pl.multiple_of(top + HALF, HALF), HALF), :]
                    scores = lax.dot_general(q, kv[h, rows, :], (((1,), (1,)), ((), ())), preferred_element_type=F32)
                    keep = lax.broadcasted_iota(jnp.int32, (HALF, BLOCK), 1) <= HALF + lax.broadcasted_iota(
                        jnp.int32, (HALF, BLOCK), 0
                    )
                    wide = jnp.concatenate([c, c], axis=1)
                    key_cum = jnp.concatenate([cum_row[b, j, pl.ds(h, 1), :] for j in range(2)], axis=1)
                    spread = jnp.where(keep, wide - key_cum, 0.0)
                    weights = jnp.where(keep, scores * jnp.exp(spread), 0.0).astype(BF16)
                    within = jnp.dot(weights, vv[h, rows, :], preferred_element_type=F32)
                    carried = jnp.dot(q, start[h, b], preferred_element_type=F32) * jnp.exp(c)
                    att[b, HALF:, pl.ds(pl.multiple_of(h * WIDTH, WIDTH), WIDTH)] = (within + carried).astype(BF16)

            ship(g, 1, *TAIL_PARTS[0])

        span = 1024
        chunks = z_count * features // span

        def gates():
            @pl.loop(0, BLOCK // 16)
            def _(i):
                rows = pl.ds(pl.multiple_of(i * 16, 16), 16)
                for j in range(chunks):
                    lanes = slice(j * span, (j + 1) * span)
                    gs[rows, lanes] = gain_ref[:, lanes] * jax.nn.sigmoid(gv[rows, lanes].astype(F32))

        def norm(r0, count):
            @pl.loop(0, count // 16)
            def _(i):
                rows = pl.ds(pl.multiple_of(r0 + i * 16, 16), 16)
                total = jnp.zeros((16, span), F32)
                for j in range(chunks):
                    wide = recv[rows, j * span : (j + 1) * span].astype(F32)
                    total = total + wide * wide
                mean = jnp.sum(total, axis=1, keepdims=True) * (1.0 / (z_count * features))
                scale = lax.rsqrt(mean + norm_eps)
                for j in range(chunks):
                    lanes = slice(j * span, (j + 1) * span)
                    recv[rows, lanes] = (recv[rows, lanes].astype(F32) * scale * gs[rows, lanes]).astype(BF16)

        def out_copy(part, r0, rows):
            return pltpu.make_async_copy(recv.at[pl.ds(r0, rows)], out_ref.at[pl.ds(r0, rows)], out_sem.at[part])

        for g in range(AHEAD):
            states(g)
        pl.semaphore_wait(barrier, 1 + (NX - 1) + (NY - 1) + (z_count - 1))
        dec_pair.start()

        @pl.loop(0, LAG_ATT + groups)
        def _(k):
            @pl.when(k < groups)
            def _():
                pair_copy(k).start()

            @pl.when(k >= LAG_ATT)
            def _():
                attend_first(k - LAG_ATT)

            @pl.when((k >= LAG_RET) & (k < LAG_RET + groups))
            def _():
                return_step(k - LAG_RET)

            @pl.when((k >= LAG_Y) & (k < LAG_Y + groups))
            def _():
                row_step(k - LAG_Y)

            @pl.when((k >= 1) & (k < 1 + groups))
            def _():
                pair_step(k - 1)

            @pl.when(k + AHEAD < groups)
            def _():
                states(k + AHEAD)

        @pl.loop(0, groups)
        def _(g):
            attend_second(g)

        for part in range(1, len(TAIL_PARTS)):
            r0, rows = TAIL_PARTS[part]

            @pl.loop(0, groups)
            def _(g):
                ship(g, part + 1, r0, rows)

        gate_copy.wait()
        gates()
        parts = ((0, HALF),) + TAIL_PARTS
        for part, (r0, rows) in enumerate(parts):
            arrived(part, r0, rows)
            norm(r0, rows)
            out_copy(part, r0, rows).start()

        dec_pair.wait_send()
        for d in range(1, NX):
            dx_copy(d).wait_send()
        for d in range(1, NY):
            dy_copy(d).wait_send()

        @pl.loop(0, groups)
        def _(g):
            pair_copy(g).wait_send()
            for d in range(1, NX):
                x_copy(g, d).wait_send()
            for d in range(1, NY):
                y_copy(g, d).wait_send()
            ret_copy(g).wait_send()
            for part, (r0, rows) in enumerate(parts):
                for d in range(1, z_count):
                    z_copy(g, part, r0, rows, d).wait_send()

        for part, (r0, rows) in enumerate(parts):
            out_copy(part, r0, rows).wait()

    return kernel


def solution(mesh):
    z_count = mesh.shape["head"]

    def on_device(queries, key_rows, value_rows, log_decay, gate_logits, norm_gain):
        local, features = queries.shape
        heads = log_decay.shape[0]
        blocks = local // BLOCK
        groups = heads // 2
        rows, wide = gate_logits.shape
        parts = 1 + len(TAIL_PARTS)
        vmem, dma = pltpu.VMEM, pltpu.SemaphoreType.DMA
        state = (WIDTH, WIDTH)
        return pl.pallas_call(
            make_kernel(heads, blocks, z_count),
            out_shape=jax.ShapeDtypeStruct((rows, wide), BF16),
            in_specs=[
                pl.BlockSpec(memory_space=pl.ANY),
                pl.BlockSpec(memory_space=pl.ANY),
                pl.BlockSpec(memory_space=pl.ANY),
                pl.BlockSpec(memory_space=pltpu.VMEM),
                pl.BlockSpec(memory_space=pl.ANY),
                pl.BlockSpec(memory_space=pltpu.VMEM),
            ],
            out_specs=pl.BlockSpec(memory_space=pl.ANY),
            scratch_shapes=[
                vmem((heads, local, WIDTH), BF16),
                vmem((heads, local, WIDTH), BF16),
                vmem((heads, local, WIDTH), BF16),
                vmem((rows, wide), BF16),
                vmem((rows, wide), F32),
                vmem((z_count, rows, features), BF16),
                vmem((rows, wide), BF16),
                vmem((blocks, 2, heads, HALF), F32),
                vmem((blocks, BLOCK, WIDTH), F32),
                vmem((heads, blocks, BLOCK, WIDTH), F32),
                vmem((heads, blocks) + state, F32),
                vmem((heads, blocks) + state, BF16),
                vmem((heads,) + state, F32),
                vmem((groups,) + state, F32),
                vmem((groups, NX) + state, BF16),
                vmem((groups, NY) + state, BF16),
                vmem((groups,) + state, F32),
                vmem((groups,) + state, F32),
                vmem((heads,) + state, F32),
                vmem((heads, WIDTH), F32),
                vmem((heads, WIDTH), F32),
                vmem((NX, heads, WIDTH), F32),
                vmem((NY, heads, WIDTH), F32),
                dma((3, heads)),
                dma,
                dma((parts,)),
                dma((parts, groups)),
                dma((groups,)),
                dma((groups,)),
                dma((groups, NX - 1)),
                dma((groups, NX - 1)),
                dma((groups, NY - 1)),
                dma((groups, NY - 1)),
                dma((groups,)),
                dma((groups,)),
                dma((parts, groups, z_count - 1)),
                dma((parts, groups, z_count - 1)),
                dma,
                dma,
                dma((NX - 1,)),
                dma((NX - 1,)),
                dma((NY - 1,)),
                dma((NY - 1,)),
            ],
            compiler_params=pltpu.CompilerParams(
                collective_id=0, has_side_effects=True, vmem_limit_bytes=56 * 2**20
            ),
        )(queries, key_rows, value_rows, log_decay, gate_logits, norm_gain[None, :])

    placed = (
        P("seq", "head"),
        P("seq", "head"),
        P("seq", "head"),
        P("head", "seq"),
        P(("seq", "head"), None),
        P(),
    )
    return jax.shard_map(
        on_device, mesh=mesh, in_specs=placed, out_specs=P(("seq", "head"), None), check_vma=False
    )
```

time: 301 us -> 105 us (0.35)
  blocking collectives: 117 us -> 0 us
  Pallas kernels: 0 us -> 99.9 us
  matrix products: 72.3 us -> 0 us
  waiting for transfers between devices: 32.9 us -> 0 us
  local copies, waits for them, and re-layouts: 36.6 us -> 4.64 us
  other arithmetic: 26.8 us -> 0 us
  between operations: 14.1 us -> 0.01 us
    pallas_call x0 -> x1, Pallas kernels: none -> 99.9 us  [on_device(): pl.pallas_call(make_kernel(heads, blocks, z_count), out_shape=jax.ShapeDt...]
    dot_general x4 -> x0, matrix products: 72.3 us -> none  [the longest x1 43.1 us: earlier_states(): jnp.einsum('ph,phde->hde', factor, shard_piece, precision=lax.Precision.H...]
    unnamed x1 -> x0, blocking collectives: 64.7 us -> none
    all_to_all x1 -> x0, blocking collectives: 52.5 us -> none  [on_device(): lax.all_to_all(attended, 'head', split_axis=0, concat_axis=1, tiled=True)]
    all_gather x1 -> x0, waiting for transfers between devices: 32.9 us -> none  [earlier_states(): shard_piece = lax.all_gather(local_total[None], 'seq', axis=0, tiled=True)]
    unnamed x18 -> x1, local copies, waits for them, and re-layouts: 19 us -> 4.64 us
    convert_element_type x2 -> x0, other arithmetic: 10.4 us -> none  [the longest x1 6.03 us: on_device(): (normed * jax.nn.sigmoid(gate_logits.astype(jnp.float32))).astype(jnp.bfl...]
    convert_element_type x1 -> x0, local copies, waits for them, and re-layouts: 8.91 us -> none  [on_device(): widened = token_major.astype(jnp.float32)]
  transfers between devices with their start and end apart: 1 -> 0, of which waited for: 1 -> 0; matrix products, arithmetic and copies ran while one was open for 7% -> 0% of each run, Pallas kernels for 0% -> 0%
where the time goes in v1:
time: 105 us
  Pallas kernels  99.9 us (95%)
  local copies, waits for them, and re-layouts  4.64 us (4%)
    pallas_call x1, Pallas kernels, on_device(): pl.pallas_call(make_kernel(heads, blocks, z_count), out_shape=jax.ShapeDt...  99.9 us
    unnamed x1, local copies, waits for them, and re-layouts  4.64 us

profile of v1, /device:TPU:1, one launch (start us, length us, event | category | flops | bytes accessed | tf_op | source)
XLA Modules:
  0.0 104.6 jit_solution(7648157699572345989)
XLA Ops:
  0.0 99.9 %shard_map.64 = bf16[256,8192]{1,0:T(8,128)(2,1)} custom-call(bf16[1024,2048]{1,0:T(8,128)(2,1)} %q_hbm.1, bf16[1024,2048]{1,0:T(8,128)(2,1)} %k_hbm.1, bf16[1024,2048]{1,0:T(8,128)(2,1)} %v_hbm.1, f32[16,1024]{1,0:T(8,128)} %ld_ref.1, bf16[256,8192]{1,0:T(8,128)(2,1)} %gate_hbm.1, f32[1,8192]{1,0:T(1,128)} %bitcast.1), custom_call_target="tpu_custom_call" | custom-call | tf_op jit(solution)/shard_map/pallas_call | solution.py:442
  99.9 4.6 %copy.8 = bf16[256,8192]{1,0:T(8,128)(2,1)} copy(bf16[256,8192]{1,0:T(8,128)(2,1)} %shard_map.64) | data formatting | bytes 8388608

commit v2 on v1

v2 whole, which is shorter than its diff:
```python
import jax
import jax.numpy as jnp
from jax import lax
from jax.experimental import pallas as pl
from jax.experimental.pallas import tpu as pltpu
from jax.sharding import PartitionSpec as P

BLOCK = 256
HALF = 128
WIDTH = 128
norm_eps = 1e-06

MESH = pl.DeviceIdType.MESH
F32 = jnp.float32
BF16 = jnp.bfloat16

NX = 4
NY = 4
AHEAD = 3
LAG_Y = 4
LAG_RET = 7
LAG_ATT = 8
TAIL_PARTS = ((128, 64), (192, 32), (224, 32))


def make_kernel(heads, blocks, z_count):
    groups = heads // 2
    features = heads * WIDTH

    def kernel(
        q_hbm, k_hbm, v_hbm, ld_hbm, gate_hbm, gain_hbm, out_ref,
        qb, kvb, gv, ld_ref, gain_ref, att, recv, cum_row, cum_col, col, loc, start, tot, pair_in, xb, yb, prow, sret, sin,
        dec, dsib, dx, dy,
        kv_sem, q_sem, ld_sem, gain_sem, gate_sem, out_sem, own_sem,
        pair_s, pair_r, x_s, x_r, y_s, y_r, ret_s, ret_r, z_s, z_r,
        dp_s, dp_r, dx_s, dx_r, dy_s, dy_r,
    ):
        seq = lax.axis_index("seq")
        z = lax.axis_index("head")
        core = lax.rem(seq, 2)
        x = lax.rem(seq // 2, NX)
        y = seq // (2 * NX)
        sibling = seq + 1 - 2 * core

        def x_peer(d):
            return (y * NX + lax.rem(x + d, NX)) * 2 + core

        def y_peer(d):
            return (lax.rem(y + d, NY) * NX + x) * 2 + core

        def z_peer(d):
            return lax.rem(z + d, z_count)

        def send(src, dst, s, r, axis, dev):
            return pltpu.make_async_remote_copy(
                src_ref=src, dst_ref=dst, send_sem=s, recv_sem=r, device_id={axis: dev}, device_id_type=MESH
            )

        def got(ref, sem):
            pltpu.make_async_copy(ref, ref, sem).wait()

        def pair_lanes(g):
            return pl.ds(pl.multiple_of(g * 2 * WIDTH, 2 * WIDTH), 2 * WIDTH)

        barrier = pltpu.get_barrier_semaphore()
        pl.semaphore_signal(barrier, inc=1, device_id={"seq": sibling}, device_id_type=MESH)
        for d in range(1, NX):
            pl.semaphore_signal(barrier, inc=1, device_id={"seq": x_peer(d)}, device_id_type=MESH)
        for d in range(1, NY):
            pl.semaphore_signal(barrier, inc=1, device_id={"seq": y_peer(d)}, device_id_type=MESH)
        for d in range(1, z_count):
            pl.semaphore_signal(barrier, inc=1, device_id={"head": z_peer(d)}, device_id_type=MESH)

        ld_copy = pltpu.make_async_copy(ld_hbm, ld_ref, ld_sem)
        ld_copy.start()

        @pl.loop(0, groups)
        def _(g):
            pltpu.make_async_copy(k_hbm.at[:, pair_lanes(g)], kvb.at[g, 0], kv_sem.at[g]).start()
            pltpu.make_async_copy(v_hbm.at[:, pair_lanes(g)], kvb.at[g, 1], kv_sem.at[g]).start()

        @pl.loop(0, groups)
        def _(g):
            pltpu.make_async_copy(q_hbm.at[:, pair_lanes(g)], qb.at[g], q_sem.at[g]).start()

        gain_copy = pltpu.make_async_copy(gain_hbm, gain_ref, gain_sem)
        gain_copy.start()
        gate_copy = pltpu.make_async_copy(gate_hbm, gv, gate_sem)
        gate_copy.start()

        t_at = lax.broadcasted_iota(jnp.int32, (BLOCK, BLOCK), 0)
        s_at = lax.broadcasted_iota(jnp.int32, (BLOCK, BLOCK), 1)
        lower = (s_at <= t_at).astype(BF16)
        upper = (t_at <= s_at).astype(BF16)

        def thirds(wide):
            pieces = []
            for _ in range(3):
                pieces.append(wide.astype(BF16))
                wide = wide - pieces[-1].astype(F32)
            return pieces

        def add_up(pieces, one):
            return one(pieces[2]) + one(pieces[1]) + one(pieces[0])

        ld_copy.wait()
        ld = thirds(jnp.concatenate([ld_ref[:, b * BLOCK : (b + 1) * BLOCK] for b in range(blocks)], axis=0))
        running = add_up(ld, lambda p: jnp.dot(p, upper, preferred_element_type=F32))
        for b in range(blocks):
            cum_row[b, 0] = running[b * heads : (b + 1) * heads, :HALF]
            cum_row[b, 1] = running[b * heads : (b + 1) * heads, HALF:]
        blank = jnp.zeros((WIDTH - blocks * heads, BLOCK), BF16)
        cum_col[...] = add_up(
            ld,
            lambda p: lax.dot_general(
                lower, jnp.concatenate([p, blank], axis=0), (((1,), (1,)), ((), ())), preferred_element_type=F32
            ),
        )
        ends = add_up(ld, lambda p: jnp.dot(p, jnp.ones((BLOCK, WIDTH), BF16), preferred_element_type=F32))
        total = ends[:heads]
        for b in range(1, blocks):
            total = total + ends[b * heads : (b + 1) * heads]
        dec[...] = total

        def states(g):
            got(kvb.at[g], kv_sem.at[g])
            runs = [jnp.zeros((WIDTH, WIDTH), F32)] * 2
            for b in range(blocks):
                rows = slice(b * BLOCK, (b + 1) * BLOCK)
                for i in range(2):
                    h = 2 * g + i
                    turned = pltpu.roll(cum_col[...], lax.rem(WIDTH - b * heads - h, WIDTH), 1)
                    c = jnp.broadcast_to(turned[:, :1], (BLOCK, WIDTH))
                    col[h, b] = c
                    end = c[BLOCK - 1 :, :]
                    weighted = (kvb[g, 0, rows, i * WIDTH : (i + 1) * WIDTH].astype(F32) * jnp.exp(end - c)).astype(BF16)
                    v = kvb[g, 1, rows, i * WIDTH : (i + 1) * WIDTH]
                    piece = lax.dot_general(weighted, v, (((0,), (0,)), ((), ())), preferred_element_type=F32)
                    loc[h, b] = runs[i]
                    runs[i] = jnp.exp(end) * runs[i] + piece
            for i in range(2):
                tot[2 * g + i] = runs[i]

        def pair_copy(g):
            return send(tot.at[2 * g + 1 - core], pair_in.at[g], pair_s, pair_r.at[g], "seq", sibling)

        def x_copy(g, d):
            return send(xb.at[g, x], xb.at[g, x], x_s, x_r.at[g], "seq", x_peer(d))

        def y_copy(g, d):
            return send(yb.at[g, y], yb.at[g, y], y_s, y_r.at[g], "seq", y_peer(d))

        def ret_copy(g):
            return send(sret.at[g], sin.at[2 * g + core], ret_s, ret_r.at[g], "seq", sibling)

        def ret_got(g):
            return send(sret.at[g], sin.at[2 * g + 1 - core], ret_s, ret_r.at[g], "seq", sibling)

        dec_pair = send(dec, dsib, dp_s, dp_r, "seq", sibling)

        def dx_copy(d):
            return send(dx.at[x], dx.at[x], dx_s, dx_r, "seq", x_peer(d))

        def dy_copy(d):
            return send(dy.at[y], dy.at[y], dy_s, dy_r, "seq", y_peer(d))

        def between(rows, lo, hi):
            total = jnp.zeros((1, WIDTH), F32)
            for i in range(lo + 1, len(rows)):
                total = total + jnp.where(i < hi, rows[i], 0.0)
            return total

        def own_core(g):
            h = 2 * g + core
            mine, other = tot[h], pair_in[g]
            here, there = dec[pl.ds(h, 1), :], dsib[pl.ds(h, 1), :]
            first = core == 0
            return (
                h,
                jnp.where(first, mine, other),
                jnp.where(first, other, mine),
                jnp.where(first, here, there),
                jnp.where(first, there, here),
            )

        def pair_step(g):
            pair_copy(g).wait_recv()

            @pl.when(g == 0)
            def _():
                dec_pair.wait_recv()
                dx[x] = dec[...] + dsib[...]
                for d in range(1, NX):
                    dx_copy(d).start()

            h, first, second, _, second_decay = own_core(g)
            xb[g, x] = (jnp.exp(second_decay) * first + second).astype(xb.dtype)
            for d in range(1, NX):
                x_copy(g, d).start()

        def x_rows(h):
            return [dx[i, pl.ds(h, 1), :] for i in range(NX)]

        def row_step(g):
            @pl.when(g == 0)
            def _():
                got(dx.at[pl.ds(0, NX - 1)], dx_r)
                dy[y] = dx[0] + dx[1] + dx[2] + dx[3]
                for d in range(1, NY):
                    dy_copy(d).start()

            got(xb.at[g, pl.ds(0, NX - 1)], x_r.at[g])
            h = 2 * g + core
            rows = x_rows(h)
            whole = jnp.zeros((WIDTH, WIDTH), F32)
            before = jnp.zeros((WIDTH, WIDTH), F32)
            for i in range(NX):
                piece = xb[g, i].astype(F32)
                whole = whole + jnp.exp(between(rows, i, NX)) * piece
                before = before + jnp.where(i < x, jnp.exp(between(rows, i, x)), 0.0) * piece
            prow[g] = before
            yb[g, y] = whole.astype(yb.dtype)
            for d in range(1, NY):
                y_copy(g, d).start()

        def return_step(g):
            @pl.when(g == 0)
            def _():
                got(dy.at[pl.ds(0, NY - 1)], dy_r)

            got(yb.at[g, pl.ds(0, NY - 1)], y_r.at[g])
            h, first, _, first_decay, _ = own_core(g)
            rows = [dy[i, pl.ds(h, 1), :] for i in range(NY)]
            above = jnp.zeros((WIDTH, WIDTH), F32)
            for i in range(NY):
                above = above + jnp.where(i < y, jnp.exp(between(rows, i, y)), 0.0) * yb[g, i].astype(F32)
            at_first = jnp.exp(between(x_rows(h), -1, x)) * above + prow[g]
            at_second = jnp.exp(first_decay) * at_first + first
            sin[h] = jnp.where(core == 0, at_first, at_second)
            sret[g] = jnp.where(core == 0, at_second, at_first)
            ret_copy(g).start()

        def z_lanes(g):
            return pl.ds(pl.multiple_of(z * features + g * 2 * WIDTH, 2 * WIDTH), 2 * WIDTH)

        def z_copy(g, part, r0, rows, d):
            p = z_peer(d)
            src = att.at[p, pl.ds(r0, rows), pair_lanes(g)]
            return send(src, recv.at[pl.ds(r0, rows), z_lanes(g)], z_s, z_r.at[part], "head", p)

        def own_copy(g, part, r0, rows):
            src = att.at[z, pl.ds(r0, rows), pair_lanes(g)]
            return pltpu.make_async_copy(src, recv.at[pl.ds(r0, rows), z_lanes(g)], own_sem.at[part])

        def ship(g, part, r0, rows):
            for d in (2, 1, 3):
                z_copy(g, part, r0, rows, d).start()
            own_copy(g, part, r0, rows).start()

        def arrived(part, r0, rows):
            got(att.at[pl.ds(0, z_count - 1), pl.ds(r0, rows)], z_r.at[part])
            got(att.at[0, pl.ds(r0, rows)], own_sem.at[part])

        def attend_first(g):
            ret_got(g).wait_recv()
            got(qb.at[g], q_sem.at[g])
            keep = lax.broadcasted_iota(jnp.int32, (HALF, HALF), 1) <= lax.broadcasted_iota(jnp.int32, (HALF, HALF), 0)
            gone = [jnp.zeros((1, WIDTH), F32)] * 2
            for b in range(blocks):
                rows = slice(b * BLOCK, b * BLOCK + HALF)
                for i in range(2):
                    h = 2 * g + i
                    c = col[h, b, :HALF, :]
                    begin = (jnp.exp(gone[i]) * sin[h] + loc[h, b]).astype(BF16)
                    start[h, b] = begin
                    lanes = slice(i * WIDTH, (i + 1) * WIDTH)
                    q = qb[g, rows, lanes]
                    scores = lax.dot_general(q, kvb[g, 0, rows, lanes], (((1,), (1,)), ((), ())), preferred_element_type=F32)
                    spread = jnp.where(keep, c - cum_row[b, 0, pl.ds(h, 1), :], 0.0)
                    weights = jnp.where(keep, scores * jnp.exp(spread), 0.0).astype(BF16)
                    within = jnp.dot(weights, kvb[g, 1, rows, lanes], preferred_element_type=F32)
                    carried = jnp.dot(q, begin, preferred_element_type=F32) * jnp.exp(c)
                    att[b, :HALF, pl.ds(pl.multiple_of(h * WIDTH, WIDTH), WIDTH)] = (within + carried).astype(BF16)
                    gone[i] = gone[i] + col[h, b, BLOCK - 1 :, :]
            ship(g, 0, 0, HALF)

        def attend_second(g):
            keep = lax.broadcasted_iota(jnp.int32, (HALF, BLOCK), 1) <= HALF + lax.broadcasted_iota(
                jnp.int32, (HALF, BLOCK), 0
            )
            for b in range(blocks):
                rows = slice(b * BLOCK, (b + 1) * BLOCK)
                for i in range(2):
                    h = 2 * g + i
                    c = col[h, b, HALF:, :]
                    lanes = slice(i * WIDTH, (i + 1) * WIDTH)
                    q = qb[g, b * BLOCK + HALF : (b + 1) * BLOCK, lanes]
                    scores = lax.dot_general(q, kvb[g, 0, rows, lanes], (((1,), (1,)), ((), ())), preferred_element_type=F32)
                    wide = jnp.concatenate([c, c], axis=1)
                    key_cum = jnp.concatenate([cum_row[b, j, pl.ds(h, 1), :] for j in range(2)], axis=1)
                    spread = jnp.where(keep, wide - key_cum, 0.0)
                    weights = jnp.where(keep, scores * jnp.exp(spread), 0.0).astype(BF16)
                    within = jnp.dot(weights, kvb[g, 1, rows, lanes], preferred_element_type=F32)
                    carried = jnp.dot(q, start[h, b], preferred_element_type=F32) * jnp.exp(c)
                    att[b, HALF:, pl.ds(pl.multiple_of(h * WIDTH, WIDTH), WIDTH)] = (within + carried).astype(BF16)

            ship(g, 1, *TAIL_PARTS[0])

        chunks = z_count * heads

        def gates():
            @pl.loop(0, BLOCK // 16)
            def _(i):
                rows = pl.ds(pl.multiple_of(i * 16, 16), 16)
                for j in range(chunks):
                    lanes = slice(j * WIDTH, (j + 1) * WIDTH)
                    col[j // blocks, j % blocks, rows, :] = gain_ref[:, lanes] * jax.nn.sigmoid(gv[rows, lanes].astype(F32))

        def norm(r0, count):
            @pl.loop(0, count // 16)
            def _(i):
                rows = pl.ds(pl.multiple_of(r0 + i * 16, 16), 16)
                sums = [jnp.zeros((16, WIDTH), F32)] * 4
                for j in range(chunks):
                    wide = recv[rows, j * WIDTH : (j + 1) * WIDTH].astype(F32)
                    sums[j % 4] = sums[j % 4] + wide * wide
                total = (sums[0] + sums[1]) + (sums[2] + sums[3])
                mean = jnp.sum(total, axis=1, keepdims=True) * (1.0 / (z_count * features))
                scale = jnp.broadcast_to(lax.rsqrt(mean + norm_eps), (16, WIDTH))
                for j in range(chunks):
                    lanes = slice(j * WIDTH, (j + 1) * WIDTH)
                    wide = recv[rows, lanes].astype(F32)
                    recv[rows, lanes] = (wide * scale * col[j // blocks, j % blocks, rows, :]).astype(BF16)

        def out_copy(part, r0, rows):
            return pltpu.make_async_copy(recv.at[pl.ds(r0, rows)], out_ref.at[pl.ds(r0, rows)], out_sem.at[part])

        for g in range(AHEAD):
            states(g)
        pl.semaphore_wait(barrier, 1 + (NX - 1) + (NY - 1) + (z_count - 1))
        dec_pair.start()

        @pl.loop(0, LAG_ATT + groups)
        def _(k):
            @pl.when(k < groups)
            def _():
                pair_copy(k).start()

            @pl.when(k >= LAG_ATT)
            def _():
                attend_first(k - LAG_ATT)

            @pl.when((k >= LAG_RET) & (k < LAG_RET + groups))
            def _():
                return_step(k - LAG_RET)

            @pl.when((k >= LAG_Y) & (k < LAG_Y + groups))
            def _():
                row_step(k - LAG_Y)

            @pl.when((k >= 1) & (k < 1 + groups))
            def _():
                pair_step(k - 1)

            @pl.when(k + AHEAD < groups)
            def _():
                states(k + AHEAD)

        @pl.loop(0, groups)
        def _(g):
            attend_second(g)

        for part in range(1, len(TAIL_PARTS)):
            r0, rows = TAIL_PARTS[part]

            @pl.loop(0, groups)
            def _(g):
                ship(g, part + 1, r0, rows)

        gain_copy.wait()
        gate_copy.wait()
        gates()
        parts = ((0, HALF),) + TAIL_PARTS
        for part, (r0, rows) in enumerate(parts):
            arrived(part, r0, rows)
            norm(r0, rows)
            out_copy(part, r0, rows).start()

        got(dec, dp_s)
        got(dx.at[pl.ds(0, NX - 1)], dx_s)
        got(dy.at[pl.ds(0, NY - 1)], dy_s)
        got(pair_in, pair_s)
        got(xb.at[:, pl.ds(0, NX - 1)], x_s)
        got(yb.at[:, pl.ds(0, NY - 1)], y_s)
        got(sret, ret_s)
        got(att.at[pl.ds(0, z_count - 1)], z_s)
        for part, (r0, rows) in enumerate(parts):
            out_copy(part, r0, rows).wait()

    return kernel


def solution(mesh):
    z_count = mesh.shape["head"]

    def on_device(queries, key_rows, value_rows, log_decay, gate_logits, norm_gain):
        local, features = queries.shape
        heads = log_decay.shape[0]
        blocks = local // BLOCK
        groups = heads // 2
        rows, wide = gate_logits.shape
        parts = 1 + len(TAIL_PARTS)
        vmem, dma = pltpu.VMEM, pltpu.SemaphoreType.DMA
        state = (WIDTH, WIDTH)
        return pl.pallas_call(
            make_kernel(heads, blocks, z_count),
            out_shape=jax.ShapeDtypeStruct((rows, wide), BF16),
            in_specs=[pl.BlockSpec(memory_space=pltpu.HBM)] * 6,
            out_specs=pl.BlockSpec(memory_space=pl.ANY),
            scratch_shapes=[
                vmem((groups, local, 2 * WIDTH), BF16),
                vmem((groups, 2, local, 2 * WIDTH), BF16),
                vmem((rows, wide), BF16),
                vmem((heads, local), F32),
                vmem((1, wide), F32),
                vmem((z_count, rows, features), BF16),
                vmem((rows, wide), BF16),
                vmem((blocks, 2, heads, HALF), F32),
                vmem((BLOCK, WIDTH), F32),
                vmem((heads, blocks, BLOCK, WIDTH), F32),
                vmem((heads, blocks) + state, F32),
                vmem((heads, blocks) + state, BF16),
                vmem((heads,) + state, F32),
                vmem((groups,) + state, F32),
                vmem((groups, NX) + state, BF16),
                vmem((groups, NY) + state, BF16),
                vmem((groups,) + state, F32),
                vmem((groups,) + state, F32),
                vmem((heads,) + state, F32),
                vmem((heads, WIDTH), F32),
                vmem((heads, WIDTH), F32),
                vmem((NX, heads, WIDTH), F32),
                vmem((NY, heads, WIDTH), F32),
                dma((groups,)),
                dma((groups,)),
                dma,
                dma,
                dma,
                dma((parts,)),
                dma((parts,)),
                dma,
                dma((groups,)),
                dma,
                dma((groups,)),
                dma,
                dma((groups,)),
                dma,
                dma((groups,)),
                dma,
                dma((parts,)),
                dma,
                dma,
                dma,
                dma,
                dma,
                dma,
            ],
            compiler_params=pltpu.CompilerParams(
                collective_id=0, has_side_effects=True, vmem_limit_bytes=46 * 2**20
            ),
        )(queries, key_rows, value_rows, log_decay, gate_logits, norm_gain[None, :])

    placed = (
        P("seq", "head"),
        P("seq", "head"),
        P("seq", "head"),
        P("head", "seq"),
        P(("seq", "head"), None),
        P(),
    )
    return jax.shard_map(
        on_device, mesh=mesh, in_specs=placed, out_specs=P(("seq", "head"), None), check_vma=False
    )
```

time: 105 us -> 76.1 us (0.72)
  Pallas kernels: 99.9 us -> 72.3 us
    pallas_call x1, Pallas kernels: 99.9 us -> 72.3 us  [on_device(): pl.pallas_call(make_kernel(heads, blocks, z_count), out_shape=jax.ShapeDt...]
    unnamed x1 -> x5, local copies, waits for them, and re-layouts: 4.64 us -> 3.61 us
where the time goes in v2:
time: 76.1 us; the launch traced here: 75.9 us
  Pallas kernels  72.3 us (95%)
  local copies, waits for them, and re-layouts  3.61 us (5%)
    pallas_call x1, Pallas kernels, on_device(): pl.pallas_call(make_kernel(heads, blocks, z_count), out_shape=jax.ShapeDt...  72.3 us
    unnamed x5, local copies, waits for them, and re-layouts  3.61 us

profile of v2, /device:TPU:1, one launch (start us, length us, event | category | flops | bytes accessed | tf_op | source)
XLA Modules:
  0.0 75.9 jit_solution(9432821601645612851)
XLA Ops:
  0.0 0.0 copy-start
  0.0 0.8 %copy-done = f32[16,1024]{1,0:T(8,128)S(1)} copy-done((f32[16,1024]{1,0:T(8,128)S(1)}, f32[16,1024]{1,0:T(8,128)}, u32[]{:S(2)}) %copy-start) | copy-done | bytes 65560
  0.8 0.0 copy-start.1
  0.8 0.8 copy-done.1
  1.6 72.3 %shard_map.64 = bf16[256,8192]{1,0:T(8,128)(2,1)S(1)} custom-call(bf16[1024,2048]{1,0:T(8,128)(2,1)} %q_hbm.1, bf16[1024,2048]{1,0:T(8,128)(2,1)} %k_hbm.1, bf16[1024,2048]{1,0:T(8,128)(2,1)} %v_hbm.1, f32[16,1024]{1,0:T(8,128)S(1)} %copy-done, bf16[256,8192]{1,0:T(8,128)(2,1)} %gate_hbm.1, f32[1,8192]{1,0:T(1,128)S(1)} %bitcast.1), custom_call_target="tpu_custom_call" | custom-call | tf_op jit(solution)/shard_map/pallas_call | solution.py:415
  73.9 2.0 %copy.8 = bf16[256,8192]{1,0:T(8,128)(2,1)} copy(bf16[256,8192]{1,0:T(8,128)(2,1)S(1)} %shard_map.64) | data formatting | bytes 8388608
Async XLA Ops:
  0.0 0.8 %copy-start = (f32[16,1024]{1,0:T(8,128)S(1)}, f32[16,1024]{1,0:T(8,128)}, u32[]{:S(2)}) copy-start(f32[16,1024]{1,0:T(8,128)} %ld_hbm.1) | copy-start | bytes 196612
  0.8 0.8 copy-start.1

commit v3 on v2

--- a/solution.py
+++ b/solution.py
@@ -16,11 +16,11 @@
 
 NX = 4
 NY = 4
-AHEAD = 3
+AHEAD = 1
 LAG_Y = 4
 LAG_RET = 7
 LAG_ATT = 8
-TAIL_PARTS = ((128, 64), (192, 32), (224, 32))
+TAIL_PARTS = ((128, 64), (192, 48), (240, 16))
 
 
 def make_kernel(heads, blocks, z_count):
@@ -30,7 +30,7 @@
     def kernel(
         q_hbm, k_hbm, v_hbm, ld_hbm, gate_hbm, gain_hbm, out_ref,
         qb, kvb, gv, ld_ref, gain_ref, att, recv, cum_row, cum_col, col, loc, start, tot, pair_in, xb, yb, prow, sret, sin,
-        dec, dsib, dx, dy,
+        dec, dsib, dx, dy, lead_first, lead_second, w_row, w_before, w_above, lead_row,
         kv_sem, q_sem, ld_sem, gain_sem, gate_sem, out_sem, own_sem,
         pair_s, pair_r, x_s, x_r, y_s, y_r, ret_s, ret_r, z_s, z_r,
         dp_s, dp_r, dx_s, dx_r, dy_s, dy_r,
@@ -105,10 +105,6 @@
 
         ld_copy.wait()
         ld = thirds(jnp.concatenate([ld_ref[:, b * BLOCK : (b + 1) * BLOCK] for b in range(blocks)], axis=0))
-        running = add_up(ld, lambda p: jnp.dot(p, upper, preferred_element_type=F32))
-        for b in range(blocks):
-            cum_row[b, 0] = running[b * heads : (b + 1) * heads, :HALF]
-            cum_row[b, 1] = running[b * heads : (b + 1) * heads, HALF:]
         blank = jnp.zeros((WIDTH - blocks * heads, BLOCK), BF16)
         cum_col[...] = add_up(
             ld,
@@ -121,6 +117,12 @@
         for b in range(1, blocks):
             total = total + ends[b * heads : (b + 1) * heads]
         dec[...] = total
+
+        def cum_rows():
+            running = add_up(ld, lambda p: jnp.dot(p, upper, preferred_element_type=F32))
+            for b in range(blocks):
+                cum_row[b, 0] = running[b * heads : (b + 1) * heads, :HALF]
+                cum_row[b, 1] = running[b * heads : (b + 1) * heads, HALF:]
 
         def states(g):
             got(kvb.at[g], kv_sem.at[g])
@@ -165,7 +167,7 @@
             return send(dy.at[y], dy.at[y], dy_s, dy_r, "seq", y_peer(d))
 
         def between(rows, lo, hi):
-            total = jnp.zeros((1, WIDTH), F32)
+            total = jnp.zeros((heads, WIDTH), F32)
             for i in range(lo + 1, len(rows)):
                 total = total + jnp.where(i < hi, rows[i], 0.0)
             return total
@@ -173,107 +175,111 @@
         def own_core(g):
             h = 2 * g + core
             mine, other = tot[h], pair_in[g]
-            here, there = dec[pl.ds(h, 1), :], dsib[pl.ds(h, 1), :]
             first = core == 0
-            return (
-                h,
-                jnp.where(first, mine, other),
-                jnp.where(first, other, mine),
-                jnp.where(first, here, there),
-                jnp.where(first, there, here),
-            )
+            return h, jnp.where(first, mine, other), jnp.where(first, other, mine)
+
+        def pair_decays():
+            got(dsib, dp_r)
+            here, there = dec[...], dsib[...]
+            dx[x] = here + there
+            for d in range(1, NX):
+                dx_copy(d).start()
+            lead_first[...] = jnp.exp(jnp.where(core == 0, here, there))
+            lead_second[...] = jnp.exp(jnp.where(core == 0, there, here))
+
+        def row_decays():
+            got(dx.at[pl.ds(0, NX - 1)], dx_r)
+            rows = [dx[i] for i in range(NX)]
+            dy[y] = rows[0] + rows[1] + rows[2] + rows[3]
+            for d in range(1, NY):
+                dy_copy(d).start()
+            for i in range(NX):
+                w_row[i] = jnp.exp(between(rows, i, NX))
+                w_before[i] = jnp.where(i < x, jnp.exp(between(rows, i, x)), 0.0)
+            lead_row[...] = jnp.exp(between(rows, -1, x))
+
+        def all_decays():
+            got(dy.at[pl.ds(0, NY - 1)], dy_r)
+            rows = [dy[i] for i in range(NY)]
+            for i in range(NY):
+                w_above[i] = jnp.where(i < y, jnp.exp(between(rows, i, y)), 0.0)
 
         def pair_step(g):
+            @pl.when(g == 0)
+            def _():
+                pair_decays()
+
             pair_copy(g).wait_recv()
-
-            @pl.when(g == 0)
-            def _():
-                dec_pair.wait_recv()
-                dx[x] = dec[...] + dsib[...]
-                for d in range(1, NX):
-                    dx_copy(d).start()
-
-            h, first, second, _, second_decay = own_core(g)
-            xb[g, x] = (jnp.exp(second_decay) * first + second).astype(xb.dtype)
+            h, first, second = own_core(g)
+            xb[g, x] = (lead_second[pl.ds(h, 1), :] * first + second).astype(xb.dtype)
             for d in range(1, NX):
                 x_copy(g, d).start()
 
-        def x_rows(h):
-            return [dx[i, pl.ds(h, 1), :] for i in range(NX)]
-
         def row_step(g):
-            @pl.when(g == 0)
-            def _():
-                got(dx.at[pl.ds(0, NX - 1)], dx_r)
-                dy[y] = dx[0] + dx[1] + dx[2] + dx[3]
-                for d in range(1, NY):
-                    dy_copy(d).start()
-
             got(xb.at[g, pl.ds(0, NX - 1)], x_r.at[g])
             h = 2 * g + core
-            rows = x_rows(h)
-            whole = jnp.zeros((WIDTH, WIDTH), F32)
-            before = jnp.zeros((WIDTH, WIDTH), F32)
-            for i in range(NX):
-                piece = xb[g, i].astype(F32)
-                whole = whole + jnp.exp(between(rows, i, NX)) * piece
-                before = before + jnp.where(i < x, jnp.exp(between(rows, i, x)), 0.0) * piece
-            prow[g] = before
-            yb[g, y] = whole.astype(yb.dtype)
+
+            def mix(weights):
+                total = weights[0, pl.ds(h, 1), :] * xb[g, 0].astype(F32)
+                for i in range(1, NX):
+                    total = total + weights[i, pl.ds(h, 1), :] * xb[g, i].astype(F32)
+                return total
+
+            yb[g, y] = mix(w_row).astype(yb.dtype)
             for d in range(1, NY):
                 y_copy(g, d).start()
+            prow[g] = mix(w_before)
 
         def return_step(g):
-            @pl.when(g == 0)
-            def _():
-                got(dy.at[pl.ds(0, NY - 1)], dy_r)
-
             got(yb.at[g, pl.ds(0, NY - 1)], y_r.at[g])
-            h, first, _, first_decay, _ = own_core(g)
-            rows = [dy[i, pl.ds(h, 1), :] for i in range(NY)]
-            above = jnp.zeros((WIDTH, WIDTH), F32)
-            for i in range(NY):
-                above = above + jnp.where(i < y, jnp.exp(between(rows, i, y)), 0.0) * yb[g, i].astype(F32)
-            at_first = jnp.exp(between(x_rows(h), -1, x)) * above + prow[g]
-            at_second = jnp.exp(first_decay) * at_first + first
-            sin[h] = jnp.where(core == 0, at_first, at_second)
+            h, first, _ = own_core(g)
+            above = w_above[0, pl.ds(h, 1), :] * yb[g, 0].astype(F32)
+            for i in range(1, NY):
+                above = above + w_above[i, pl.ds(h, 1), :] * yb[g, i].astype(F32)
+            at_first = lead_row[pl.ds(h, 1), :] * above + prow[g]
+            at_second = lead_first[pl.ds(h, 1), :] * at_first + first
             sret[g] = jnp.where(core == 0, at_second, at_first)
             ret_copy(g).start()
-
-        def z_lanes(g):
-            return pl.ds(pl.multiple_of(z * features + g * 2 * WIDTH, 2 * WIDTH), 2 * WIDTH)
-
-        def z_copy(g, part, r0, rows, d):
+            sin[h] = jnp.where(core == 0, at_first, at_second)
+
+        def z_copy(lanes, part, r0, rows, d):
+            at, count = lanes
             p = z_peer(d)
-            src = att.at[p, pl.ds(r0, rows), pair_lanes(g)]
-            return send(src, recv.at[pl.ds(r0, rows), z_lanes(g)], z_s, z_r.at[part], "head", p)
-
-        def own_copy(g, part, r0, rows):
-            src = att.at[z, pl.ds(r0, rows), pair_lanes(g)]
-            return pltpu.make_async_copy(src, recv.at[pl.ds(r0, rows), z_lanes(g)], own_sem.at[part])
+            src = att.at[p, pl.ds(r0, rows), pl.ds(pl.multiple_of(at, count), count)]
+            dst = recv.at[pl.ds(r0, rows), pl.ds(pl.multiple_of(z * features + at, count), count)]
+            return send(src, dst, z_s, z_r.at[part], "head", p)
+
+        def own_copy(lanes, part, r0, rows):
+            at, count = lanes
+            src = att.at[z, pl.ds(r0, rows), pl.ds(pl.multiple_of(at, count), count)]
+            dst = recv.at[pl.ds(r0, rows), pl.ds(pl.multiple_of(z * features + at, count), count)]
+            return pltpu.make_async_copy(src, dst, own_sem.at[part])
 
         def ship(g, part, r0, rows):
+            lanes = (g * 2 * WIDTH, 2 * WIDTH)
             for d in (2, 1, 3):
-                z_copy(g, part, r0, rows, d).start()
-            own_copy(g, part, r0, rows).start()
+                z_copy(lanes, part, r0, rows, d).start()
+            own_copy(lanes, part, r0, rows).start()
 
         def arrived(part, r0, rows):
             got(att.at[pl.ds(0, z_count - 1), pl.ds(r0, rows)], z_r.at[part])
             got(att.at[0, pl.ds(r0, rows)], own_sem.at[part])
 
         def attend_first(g):
-            ret_got(g).wait_recv()
             got(qb.at[g], q_sem.at[g])
             keep = lax.broadcasted_iota(jnp.int32, (HALF, HALF), 1) <= lax.broadcasted_iota(jnp.int32, (HALF, HALF), 0)
-            gone = [jnp.zeros((1, WIDTH), F32)] * 2
-            for b in range(blocks):
-                rows = slice(b * BLOCK, b * BLOCK + HALF)
-                for i in range(2):
-                    h = 2 * g + i
+            for i in (core, 1 - core):
+                if i is not core:
+                    ret_got(g).wait_recv()
+                h = 2 * g + i
+                gone = jnp.zeros((1, WIDTH), F32)
+                lanes = pl.ds(pl.multiple_of(i * WIDTH, WIDTH), WIDTH)
+                for b in range(blocks):
+                    begin = (jnp.exp(gone) * sin[h] + loc[h, b]).astype(BF16)
+                    start[h, b] = begin
+                    gone = gone + col[h, b, BLOCK - 1 :, :]
+                    rows = slice(b * BLOCK, b * BLOCK + HALF)
                     c = col[h, b, :HALF, :]
-                    begin = (jnp.exp(gone[i]) * sin[h] + loc[h, b]).astype(BF16)
-                    start[h, b] = begin
-                    lanes = slice(i * WIDTH, (i + 1) * WIDTH)
                     q = qb[g, rows, lanes]
                     scores = lax.dot_general(q, kvb[g, 0, rows, lanes], (((1,), (1,)), ((), ())), preferred_element_type=F32)
                     spread = jnp.where(keep, c - cum_row[b, 0, pl.ds(h, 1), :], 0.0)
@@ -281,8 +287,10 @@
                     within = jnp.dot(weights, kvb[g, 1, rows, lanes], preferred_element_type=F32)
                     carried = jnp.dot(q, begin, preferred_element_type=F32) * jnp.exp(c)
                     att[b, :HALF, pl.ds(pl.multiple_of(h * WIDTH, WIDTH), WIDTH)] = (within + carried).astype(BF16)
-                    gone[i] = gone[i] + col[h, b, BLOCK - 1 :, :]
-            ship(g, 0, 0, HALF)
+                head_lanes = (h * WIDTH, WIDTH)
+                for d in (2, 1, 3):
+                    z_copy(head_lanes, 0, 0, HALF, d).start()
+                own_copy(head_lanes, 0, 0, HALF).start()
 
         def attend_second(g):
             keep = lax.broadcasted_iota(jnp.int32, (HALF, BLOCK), 1) <= HALF + lax.broadcasted_iota(
@@ -366,6 +374,18 @@
             def _():
                 states(k + AHEAD)
 
+            @pl.when(k == 1)
+            def _():
+                cum_rows()
+
+            @pl.when(k == LAG_Y - 1)
+            def _():
+                row_decays()
+
+            @pl.when(k == LAG_RET - 1)
+            def _():
+                all_decays()
+
         @pl.loop(0, groups)
         def _(g):
             attend_second(g)
@@ -412,6 +432,7 @@
         parts = 1 + len(TAIL_PARTS)
         vmem, dma = pltpu.VMEM, pltpu.SemaphoreType.DMA
         state = (WIDTH, WIDTH)
+        given = (queries, key_rows, value_rows, log_decay, gate_logits, norm_gain[None, :])
         return pl.pallas_call(
             make_kernel(heads, blocks, z_count),
             out_shape=jax.ShapeDtypeStruct((rows, wide), BF16),
@@ -441,6 +462,12 @@
                 vmem((heads, WIDTH), F32),
                 vmem((NX, heads, WIDTH), F32),
                 vmem((NY, heads, WIDTH), F32),
+                vmem((heads, WIDTH), F32),
+                vmem((heads, WIDTH), F32),
+                vmem((NX, heads, WIDTH), F32),
+                vmem((NX, heads, WIDTH), F32),
+                vmem((NY, heads, WIDTH), F32),
+                vmem((heads, WIDTH), F32),
                 dma((groups,)),
                 dma((groups,)),
                 dma,
@@ -468,7 +495,7 @@
             compiler_params=pltpu.CompilerParams(
                 collective_id=0, has_side_effects=True, vmem_limit_bytes=46 * 2**20
             ),
-        )(queries, key_rows, value_rows, log_decay, gate_logits, norm_gain[None, :])
+        )(*[pltpu.with_memory_space_constraint(a, pltpu.HBM) for a in given])
 
     placed = (
         P("seq", "head"),

time: 76.1 us -> 69.6 us (0.915)
  Pallas kernels: 72.3 us -> 67.4 us
  local copies, waits for them, and re-layouts: 3.61 us -> 2.02 us
    pallas_call x1, Pallas kernels: 72.3 us -> 67.4 us  [on_device(): pl.pallas_call(make_kernel(heads, blocks, z_count), out_shape=jax.ShapeDt...]
    unnamed x5 -> x1, local copies, waits for them, and re-layouts: 3.61 us -> 2.02 us
where the time goes in v3:
time: 69.6 us; the launch traced here: 69.5 us
  Pallas kernels  67.4 us (97%)
  local copies, waits for them, and re-layouts  2.02 us (3%)
    pallas_call x1, Pallas kernels, on_device(): pl.pallas_call(make_kernel(heads, blocks, z_count), out_shape=jax.ShapeDt...  67.4 us
    unnamed x1, local copies, waits for them, and re-layouts  2.02 us

profile of v3, /device:TPU:1, one launch (start us, length us, event | category | flops | bytes accessed | tf_op | source)
XLA Modules:
  0.0 69.5 jit_solution(11655649173088572107)
XLA Ops:
  0.0 67.4 %shard_map.64 = bf16[256,8192]{1,0:T(8,128)(2,1)S(1)} custom-call(bf16[1024,2048]{1,0:T(8,128)(2,1)} %q_hbm.1, bf16[1024,2048]{1,0:T(8,128)(2,1)} %k_hbm.1, bf16[1024,2048]{1,0:T(8,128)(2,1)} %v_hbm.1, f32[16,1024]{1,0:T(8,128)} %ld_hbm.1, bf16[256,8192]{1,0:T(8,128)(2,1)} %gate_hbm.1, f32[1,8192]{1,0:T(1,128)} %bitcast.1), custom_call_target="tpu_custom_call" | custom-call | tf_op jit(solution)/shard_map/pallas_call | solution.py:436
  67.4 2.0 %copy.8 = bf16[256,8192]{1,0:T(8,128)(2,1)} copy(bf16[256,8192]{1,0:T(8,128)(2,1)S(1)} %shard_map.64) | data formatting | bytes 8388608

commit v4 on v3

--- a/solution.py
+++ b/solution.py
@@ -20,6 +20,7 @@
 LAG_Y = 4
 LAG_RET = 7
 LAG_ATT = 8
+EARLY = 1
 TAIL_PARTS = ((128, 64), (192, 48), (240, 16))
 
 
@@ -30,10 +31,10 @@
     def kernel(
         q_hbm, k_hbm, v_hbm, ld_hbm, gate_hbm, gain_hbm, out_ref,
         qb, kvb, gv, ld_ref, gain_ref, att, recv, cum_row, cum_col, col, loc, start, tot, pair_in, xb, yb, prow, sret, sin,
-        dec, dsib, dx, dy, lead_first, lead_second, w_row, w_before, w_above, lead_row,
+        dec, dsib, dx, dy, lead_first, lead_second, w_row, w_before, w_above, lead_row, q_out, q_in, state_out, state_in,
         kv_sem, q_sem, ld_sem, gain_sem, gate_sem, out_sem, own_sem,
         pair_s, pair_r, x_s, x_r, y_s, y_r, ret_s, ret_r, z_s, z_r,
-        dp_s, dp_r, dx_s, dx_r, dy_s, dy_r,
+        dp_s, dp_r, dx_s, dx_r, dy_s, dy_r, qz_s, qz_r, qz_own, sz_s, sz_r,
     ):
         seq = lax.axis_index("seq")
         z = lax.axis_index("head")
@@ -261,9 +262,81 @@
                 z_copy(lanes, part, r0, rows, d).start()
             own_copy(lanes, part, r0, rows).start()
 
+        rest = pl.ds(0, (groups - 1) * 2 * WIDTH)
+        early_part = 1 + len(TAIL_PARTS)
+        early_lanes = (EARLY * 2 * WIDTH, 2 * WIDTH)
+
+        def early_query(d):
+            return send(q_out.at[z_peer(d)], q_in.at[z], qz_s, qz_r, "head", z_peer(d))
+
+        def early_own():
+            return pltpu.make_async_copy(q_out.at[z], q_in.at[z], qz_own)
+
+        def late_state(d):
+            return send(state_out, state_in.at[z], sz_s, sz_r, "head", z_peer(d))
+
+        def early_attend():
+            got(qb.at[EARLY], q_sem.at[EARLY])
+            for i in range(2):
+                h = 2 * EARLY + i
+                lanes = slice(i * WIDTH, (i + 1) * WIDTH)
+                gone = jnp.zeros((1, WIDTH), F32)
+                for b in range(blocks):
+                    begin = loc[h, b].astype(BF16)
+                    for half in range(2):
+                        count = (half + 1) * HALF
+                        keys = slice(b * BLOCK, b * BLOCK + count)
+                        mine = slice(half * HALF, count)
+                        c = col[h, b, mine, :]
+                        q = qb[EARLY, b * BLOCK + half * HALF : b * BLOCK + count, lanes]
+                        scores = lax.dot_general(
+                            q, kvb[EARLY, 0, keys, lanes], (((1,), (1,)), ((), ())), preferred_element_type=F32
+                        )
+                        keep = lax.broadcasted_iota(jnp.int32, (HALF, count), 1) <= half * HALF + (
+                            lax.broadcasted_iota(jnp.int32, (HALF, count), 0)
+                        )
+                        wide = jnp.concatenate([c] * (half + 1), axis=1)
+                        key_cum = jnp.concatenate([cum_row[b, j, h : h + 1, :] for j in range(half + 1)], axis=1)
+                        spread = jnp.where(keep, wide - key_cum, 0.0)
+                        weights = jnp.where(keep, scores * jnp.exp(spread), 0.0).astype(BF16)
+                        within = jnp.dot(weights, kvb[EARLY, 1, keys, lanes], preferred_element_type=F32)
+                        carried = jnp.dot(q, begin, preferred_element_type=F32) * jnp.exp(c)
+                        att[b, mine, h * WIDTH : (h + 1) * WIDTH] = (within + carried).astype(BF16)
+                        q_out[b, mine, lanes] = (q.astype(F32) * jnp.exp(c + gone)).astype(BF16)
+                    gone = gone + col[h, b, BLOCK - 1 :, :]
+            for d in (2, 1, 3):
+                z_copy(early_lanes, early_part, 0, BLOCK, d).start()
+                early_query(d).start()
+            own_copy(early_lanes, early_part, 0, BLOCK).start()
+            early_own().start()
+
+        def late_states():
+            ret_got(EARLY).wait_recv()
+            for i in range(2):
+                state_out[i] = sin[2 * EARLY + i].astype(BF16)
+            state_in[z] = state_out[...]
+            for d in (2, 1, 3):
+                late_state(d).start()
+
+        def finish_early():
+            first = pl.ds(0, 2 * WIDTH)
+            got(att.at[pl.ds(0, z_count - 1), :, first], z_r.at[early_part])
+            got(att.at[0, :, first], own_sem.at[early_part])
+            got(q_in.at[pl.ds(0, z_count - 1)], qz_r)
+            early_own().wait()
+            got(state_in.at[pl.ds(0, z_count - 1)], sz_r)
+            for source in range(z_count):
+                for i in range(2):
+                    at = source * features + (2 * EARLY + i) * WIDTH
+                    lanes = slice(at, at + WIDTH)
+                    more = jnp.dot(
+                        q_in[source, :, i * WIDTH : (i + 1) * WIDTH], state_in[source, i], preferred_element_type=F32
+                    )
+                    recv[:, lanes] = (recv[:, lanes].astype(F32) + more).astype(BF16)
+
         def arrived(part, r0, rows):
-            got(att.at[pl.ds(0, z_count - 1), pl.ds(r0, rows)], z_r.at[part])
-            got(att.at[0, pl.ds(r0, rows)], own_sem.at[part])
+            got(att.at[pl.ds(0, z_count - 1), pl.ds(r0, rows), rest], z_r.at[part])
+            got(att.at[0, pl.ds(r0, rows), rest], own_sem.at[part])
 
         def attend_first(g):
             got(qb.at[g], q_sem.at[g])
@@ -345,6 +418,7 @@
 
         for g in range(AHEAD):
             states(g)
+        cum_rows()
         pl.semaphore_wait(barrier, 1 + (NX - 1) + (NY - 1) + (z_count - 1))
         dec_pair.start()
 
@@ -354,7 +428,11 @@
             def _():
                 pair_copy(k).start()
 
-            @pl.when(k >= LAG_ATT)
+            @pl.when(k == LAG_ATT + EARLY)
+            def _():
+                late_states()
+
+            @pl.when((k >= LAG_ATT) & (k != LAG_ATT + EARLY))
             def _():
                 attend_first(k - LAG_ATT)
 
@@ -370,13 +448,13 @@
             def _():
                 pair_step(k - 1)
 
+            @pl.when(k == 1)
+            def _():
+                early_attend()
+
             @pl.when(k + AHEAD < groups)
             def _():
                 states(k + AHEAD)
-
-            @pl.when(k == 1)
-            def _():
-                cum_rows()
 
             @pl.when(k == LAG_Y - 1)
             def _():
@@ -388,18 +466,23 @@
 
         @pl.loop(0, groups)
         def _(g):
-            attend_second(g)
+            @pl.when(g != EARLY)
+            def _():
+                attend_second(g)
 
         for part in range(1, len(TAIL_PARTS)):
             r0, rows = TAIL_PARTS[part]
 
             @pl.loop(0, groups)
             def _(g):
-                ship(g, part + 1, r0, rows)
+                @pl.when(g != EARLY)
+                def _():
+                    ship(g, part + 1, r0, rows)
 
         gain_copy.wait()
         gate_copy.wait()
         gates()
+        finish_early()
         parts = ((0, HALF),) + TAIL_PARTS
         for part, (r0, rows) in enumerate(parts):
             arrived(part, r0, rows)
@@ -414,6 +497,8 @@
         got(yb.at[:, pl.ds(0, NY - 1)], y_s)
         got(sret, ret_s)
         got(att.at[pl.ds(0, z_count - 1)], z_s)
+        got(q_out.at[pl.ds(0, z_count - 1)], qz_s)
+        got(state_in.at[pl.ds(0, z_count - 1)], sz_s)
         for part, (r0, rows) in enumerate(parts):
             out_copy(part, r0, rows).wait()
 
@@ -468,13 +553,17 @@
                 vmem((NX, heads, WIDTH), F32),
                 vmem((NY, heads, WIDTH), F32),
                 vmem((heads, WIDTH), F32),
+                vmem((z_count, rows, 2 * WIDTH), BF16),
+                vmem((z_count, rows, 2 * WIDTH), BF16),
+                vmem((2,) + state, BF16),
+                vmem((z_count, 2) + state, BF16),
                 dma((groups,)),
                 dma((groups,)),
                 dma,
                 dma,
                 dma,
                 dma((parts,)),
-                dma((parts,)),
+                dma((parts + 1,)),
                 dma,
                 dma((groups,)),
                 dma,
@@ -484,7 +573,12 @@
                 dma,
                 dma((groups,)),
                 dma,
-                dma((parts,)),
+                dma((parts + 1,)),
+                dma,
+                dma,
+                dma,
+                dma,
+                dma,
                 dma,
                 dma,
                 dma,
@@ -493,7 +587,7 @@
                 dma,
             ],
             compiler_params=pltpu.CompilerParams(
-                collective_id=0, has_side_effects=True, vmem_limit_bytes=46 * 2**20
+                collective_id=0, has_side_effects=True, vmem_limit_bytes=48 * 2**20
             ),
         )(*[pltpu.with_memory_space_constraint(a, pltpu.HBM) for a in given])
 

time: 69.6 us -> 68.6 us (0.986)
  Pallas kernels: 67.4 us -> 66.5 us
    pallas_call x1, Pallas kernels: 67.4 us -> 66.5 us  [on_device(): pl.pallas_call(make_kernel(heads, blocks, z_count), out_shape=jax.ShapeDt...]
where the time goes in v4:
time: 68.6 us; the launch traced here: 68.5 us
  Pallas kernels  66.5 us (97%)
  local copies, waits for them, and re-layouts  2.02 us (3%)
    pallas_call x1, Pallas kernels, on_device(): pl.pallas_call(make_kernel(heads, blocks, z_count), out_shape=jax.ShapeDt...  66.5 us
    unnamed x1, local copies, waits for them, and re-layouts  2.02 us

profile of v4, /device:TPU:1, one launch (start us, length us, event | category | flops | bytes accessed | tf_op | source)
XLA Modules:
  0.0 68.5 jit_solution(7402833608514685012)
XLA Ops:
  0.0 66.5 %shard_map.64 = bf16[256,8192]{1,0:T(8,128)(2,1)S(1)} custom-call(bf16[1024,2048]{1,0:T(8,128)(2,1)} %q_hbm.1, bf16[1024,2048]{1,0:T(8,128)(2,1)} %k_hbm.1, bf16[1024,2048]{1,0:T(8,128)(2,1)} %v_hbm.1, f32[16,1024]{1,0:T(8,128)} %ld_hbm.1, bf16[256,8192]{1,0:T(8,128)(2,1)} %gate_hbm.1, f32[1,8192]{1,0:T(1,128)} %bitcast.1), custom_call_target="tpu_custom_call" | custom-call | tf_op jit(solution)/shard_map/pallas_call | solution.py:521
  66.5 2.0 %copy.8 = bf16[256,8192]{1,0:T(8,128)(2,1)} copy(bf16[256,8192]{1,0:T(8,128)(2,1)S(1)} %shard_map.64) | data formatting | bytes 8388608
